TPU v7x, 32 devices: a whole 2x2x4 slice. The times are simulated.
32 devices in a mesh: grp: 4 (over y, x), col: 8 (over z, core).
Axes of the slice: x: 2, y: 2, z: 4, core: 2. Of those that a mesh axis runs over, the one named last changes fastest.
Arguments:
- blocks: bfloat16 [6144, 32, 1024], P(('grp', 'col'))
- i_index: int32 [6144], P(('grp', 'col')), may hold values from 0 to 15
- j_index: int32 [6144], P(('grp', 'col')), may hold values from 0 to 63
- k_index: int32 [6144], P(('grp', 'col')), may hold values from 0 to 15
- block_count: int32 [32], P(('grp', 'col')), may hold values from 24 to 192, as said below
- b_factor: float32 [16384, 256], P(('grp', 'col'))
- c_factor: float32 [4096, 256], P(('grp', 'col'))
Outputs:
- a_update: float32 [2048, 256], P(('grp', 'col'))
- b_update: float32 [16384, 256], P(('grp', 'col'))
Inputs may be any that keep to these rules, and one draw needn't show every extreme that they name: block_count[d] is the number of live slots of device d = 8 * (grp index) + (col index): its slots d * 192 to d * 192 + block_count[d] - 1; every other slot is ignored. Some device has exactly 192 live slots.
All inputs are finite; a program needn't handle non-finite values.
Results may differ from a plain program's by a relative error of at most 0.005.
The roundings to bfloat16 on the way count: a program that leaves them out, or rounds other values in their place, can miss the bound.
Values may be sent and summed in bfloat16 or wider, within the bound.
A program may use at most 128 MiB of HBM per device.

v0:
```python
import jax
import jax.numpy as jnp
from jax import lax
from jax.sharding import PartitionSpec as P

A_DEV = 2


def solve_rows(gram, right_side):
    factor_low = lax.linalg.cholesky(gram)
    halfway = lax.linalg.triangular_solve(
        factor_low, right_side, left_side=False, lower=True, transpose_a=True
    )
    return lax.linalg.triangular_solve(
        factor_low, halfway, left_side=False, lower=True, transpose_a=False
    )


def mode_term(
    blocks,
    left_rows,
    left_index,
    tail_rows,
    tail_index,
    target_index,
    live_mask,
    targets,
    first_mode,
):
    block_edge = blocks.shape[1]
    rank_width = left_rows.shape[1]
    group_size = 16
    groups = blocks.shape[0] // group_size
    left_table = left_rows.reshape(-1, block_edge, rank_width)
    tail_table = tail_rows.reshape(-1, block_edge, rank_width)
    target_ids = jnp.arange(targets, dtype=jnp.int32)

    def one_step(running, inputs):
        tensor_group, left_idx, tail_idx, target_idx, alive_row = inputs
        left_blk = left_table[left_idx].astype(jnp.float32)
        tail_blk = tail_table[tail_idx].astype(jnp.float32)
        product = (left_blk[:, :, None, :] * tail_blk[:, None, :, :]).astype(jnp.bfloat16)
        if first_mode:
            result = jnp.einsum(
                "bim,bmr->bir",
                tensor_group,
                product.reshape(group_size, block_edge * block_edge, rank_width),
                preferred_element_type=jnp.float32,
            )
        else:
            result = jnp.einsum(
                "bijk,bikr->bjr",
                tensor_group.reshape(group_size, block_edge, block_edge, block_edge),
                product,
                preferred_element_type=jnp.float32,
            )
        select = (target_idx[None, :] == target_ids[:, None]).astype(jnp.float32) * alive_row[
            None, :
        ]
        update = jnp.dot(
            select,
            result.reshape(group_size, block_edge * rank_width),
            precision=lax.Precision.HIGHEST,
        )
        return (running + update, None)

    inputs = (
        blocks.reshape(groups, group_size, block_edge, block_edge * block_edge),
        left_index.reshape(groups, group_size),
        tail_index.reshape(groups, group_size),
        target_index.reshape(groups, group_size),
        live_mask.reshape(groups, group_size),
    )
    start_value = jnp.zeros((targets, block_edge * rank_width), jnp.float32)
    running, _ = lax.scan(one_step, start_value, inputs)
    return running.reshape(targets * block_edge, rank_width)


def on_device(blocks, i_index, j_index, k_index, block_count, b_factor, c_factor):
    highest = lax.Precision.HIGHEST
    block_edge = blocks.shape[1]
    gram_second, gram_third = lax.psum(
        (
            jnp.dot(b_factor.T, b_factor, precision=highest),
            jnp.dot(c_factor.T, c_factor, precision=highest),
        ),
        ("grp", "col"),
    )
    b_range, c_range = (
        lax.all_gather(b_factor.astype(jnp.bfloat16), "grp", axis=0, tiled=True),
        lax.all_gather(c_factor.astype(jnp.bfloat16), "grp", axis=0, tiled=True),
    )
    live_mask = (jnp.arange(blocks.shape[0], dtype=jnp.int32) < block_count[0]).astype(jnp.float32)
    first_targets = A_DEV * lax.axis_size("col")
    second_targets = b_range.shape[0] // block_edge
    partial_value = mode_term(
        blocks, b_range, j_index, c_range, k_index, i_index, live_mask, first_targets, True
    )
    gram_one = gram_second * gram_third
    whole_sum = lax.psum(partial_value, "col")
    a_whole = solve_rows(gram_one, whole_sum)
    gram_first = lax.psum(jnp.dot(a_whole.T, a_whole, precision=highest), "grp")
    col_norm = jnp.sqrt(jnp.diagonal(gram_first) + 1e-06)
    a_range = (a_whole / col_norm[None, :]).astype(jnp.bfloat16)
    own_rows = A_DEV * block_edge
    a_update = lax.dynamic_slice_in_dim(a_whole, lax.axis_index("col") * own_rows, own_rows, 0)
    gram_two = gram_first / (col_norm[:, None] * col_norm[None, :]) * gram_third
    partial_two = mode_term(
        blocks, a_range, i_index, c_range, k_index, j_index, live_mask, second_targets, False
    )
    own_two = lax.psum_scatter(partial_two, "grp", scatter_dimension=0, tiled=True)
    b_update = solve_rows(gram_two, own_two)
    return (a_update, b_update)


def solution(mesh):
    return jax.shard_map(
        on_device,
        mesh=mesh,
        in_specs=(
            P(("grp", "col"), None, None),
            P(("grp", "col")),
            P(("grp", "col")),
            P(("grp", "col")),
            P(("grp", "col")),
            P(("grp", "col"), None),
            P(("grp", "col"), None),
        ),
        out_specs=(P(("grp", "col"), None), P(("grp", "col"), None)),
        check_vma=False,
    )
```

profile of v0, /device:TPU:9, one launch (start us, length us, event | category | flops | bytes accessed | tf_op | source)
XLA Modules:
  0.0 675.8 jit_solution(17725274769278915675)
XLA Ops:
  8.0 3.0 fusion.60
  18.9 7.1 %all_gather.7 = bf16[512,256]{1,0:T(8,128)(2,1)S(1)} all-gather(bf16[128,256]{1,0:T(8,128)(2,1)S(1)} %convert_element_type.55), channel_id=1, replica_groups=mesh['grp'=4,'col'=8] {'grp'}, dimensions={0}, use_global_device_ids=true | all-gather | bytes 327680 | tf_op jit(solution)/shard_map/all_gather | solution.py:91
  26.0 117.0 %all-reduce.10.cloned.1.call-done = (f32[256,256]{0,1:T(8,128)}, f32[256,256]{0,1:T(8,128)}) async-done(((f32[256,256]{0,1:T(8,128)}, f32[256,256]{0,1:T(8,128)}), (f32[256,256]{0,1:T(8,128)}, f32[256,256]{0,1:T(8,128)})) %all-reduce.10.cloned.1.call-update) | async-done | bytes 524304 | tf_op jit(solution)/shard_map/psum | solution.py:82
  144.2 11.7 %custom-call.25 = f32[128,128]{1,0:T(8,128)S(1)} custom-call(f32[128,128]{1,0:T(8,128)S(1)} %slice.125), custom_call_target="Cholesky" | custom-call | tf_op jit(solution)/shard_map/cholesky/custom-call.2 | solution.py:10
  155.9 9.8 %custom-call.26 = f32[1,128,128]{1,2,0:T(8,128)S(1)} custom-call(f32[1,128,128]{2,1,0:T(8,128)S(1)} %get-tuple-element.289), custom_call_target="InvertDiagBlocksLowerTriangular" | custom-call | tf_op jit(solution)/shard_map/cholesky/custom-call.5 | solution.py:10
  166.4 11.7 %custom-call.27 = f32[128,128]{1,0:T(8,128)S(1)} custom-call(f32[128,128]{1,0:T(8,128)S(1)} %convolution_subtract_fusion.5), custom_call_target="Cholesky" | custom-call | tf_op jit(solution)/shard_map/cholesky/custom-call.3 | solution.py:10
  180.3 121.4 %while.30 = (s32[]{:T(128)}, f32[16,8192]{1,0:T(8,128)S(1)}, s32[12,16]{1,0:T(8,128)S(1)}, f32[12,16]{1,0:T(8,128)S(1)}, bf16[12,16,32,1024]{3,2,1,0:T(8,128)(2,...) while((s32[]{:T(128)}, f32[16,8192]{1,0:T(8,128)S(1)}, ...), condition=%wide.region_7.9_spmd.clone, body=%wide.region_6.8_spmd.clone.sunk | while | flops 302516832 | bytes 24650764 | solution.py:75
  183.1 3.9 multiply_convert_fusion.5
  193.2 3.9 multiply_convert_fusion.5
  197.1 2.7 fusion.106
  203.3 3.9 multiply_convert_fusion.5
  207.2 2.7 fusion.106
  213.4 3.9 multiply_convert_fusion.5
  217.3 2.7 fusion.106
  223.5 3.9 multiply_convert_fusion.5
  227.4 2.7 fusion.106
  233.6 3.9 multiply_convert_fusion.5
  237.5 2.7 fusion.106
  243.7 3.9 multiply_convert_fusion.5
  247.6 2.7 fusion.106
  253.8 3.9 multiply_convert_fusion.5
  257.7 2.7 fusion.106
  263.9 3.9 multiply_convert_fusion.5
  267.7 2.7 fusion.106
  274.0 3.9 multiply_convert_fusion.5
  277.8 2.7 fusion.106
  284.1 3.9 multiply_convert_fusion.5
  287.9 2.7 fusion.106
  294.2 3.9 multiply_convert_fusion.5
  298.0 2.7 fusion.106
  302.8 4.1 while.32
  306.9 19.7 %custom-call.28 = f32[2,128,128]{1,2,0:T(8,128)S(1)} custom-call(f32[2,128,128]{2,1,0:T(8,128)S(1)} %get-tuple-element.203), custom_call_target="InvertDiagBlocksLowerTriangular" | custom-call | tf_op jit(solution)/shard_map/triangular_solve/custom-call.0 | solution.py:11
  326.6 31.0 %all-reduce.6.cloned.1.call-done = f32[512,256]{1,0:T(8,128)} async-done(((f32[512,256]{1,0:T(8,128)}), f32[512,256]{1,0:T(8,128)}) %all-reduce.6.cloned.1.call-update) | async-done | bytes 524304 | tf_op jit(solution)/shard_map/psum | solution.py:100
  363.6 43.4 %all-reduce.8.cloned.1.call-done = f32[256,256]{0,1:T(8,128)} async-done(((f32[256,256]{0,1:T(8,128)}), f32[256,256]{0,1:T(8,128)}) %all-reduce.8.cloned.1.call-update) | async-done | bytes 262160 | tf_op jit(solution)/shard_map/psum | solution.py:102
  410.6 186.5 %while.31 = (s32[]{:T(128)}, f32[64,8192]{1,0:T(8,128)S(1)}, s32[12,16]{1,0:T(8,128)S(1)}, f32[12,16]{1,0:T(8,128)S(1)}, bf16[12,16,32,1024]{3,2,1,0:T(8,128)(2,...) while((s32[]{:T(128)}, f32[64,8192]{1,0:T(8,128)S(1)}, ...), condition=%wide.region_11.15_spmd.clone, body=%wide.region_10.14_spmd.clone.sunk | while | flops 378802272 | bytes 15213583 | solution.py:75
  422.8 4.4 reshape.355
  429.4 4.0 fusion.113
  437.4 4.4 reshape.355
  444.0 4.0 fusion.113
  452.1 4.4 reshape.355
  458.7 4.0 fusion.113
  466.7 4.4 reshape.355
  473.3 4.0 fusion.113
  481.3 4.4 reshape.355
  487.9 4.0 fusion.113
  496.0 4.4 reshape.355
  502.6 4.0 fusion.113
  510.6 4.4 reshape.355
  517.2 4.0 fusion.113
  525.3 4.4 reshape.355
  531.9 4.0 fusion.113
  539.9 4.4 reshape.355
  546.5 4.0 fusion.113
  554.5 4.4 reshape.355
  561.1 4.0 fusion.113
  569.2 4.4 reshape.355
  575.8 4.0 fusion.113
  583.8 4.4 reshape.355
  590.4 4.0 fusion.113
  601.9 11.7 %custom-call.30 = f32[128,128]{1,0:T(8,128)S(1)} custom-call(f32[128,128]{1,0:T(8,128)S(1)} %slice.133), custom_call_target="Cholesky" | custom-call | tf_op jit(solution)/shard_map/cholesky/custom-call.2 | solution.py:10
  613.6 9.8 %custom-call.31 = f32[1,128,128]{1,2,0:T(8,128)S(1)} custom-call(f32[1,128,128]{2,1,0:T(8,128)S(1)} %get-tuple-element.285), custom_call_target="InvertDiagBlocksLowerTriangular" | custom-call | tf_op jit(solution)/shard_map/cholesky/custom-call.5 | solution.py:10
  624.1 11.7 %custom-call.32 = f32[128,128]{1,0:T(8,128)S(1)} custom-call(f32[128,128]{1,0:T(8,128)S(1)} %convolution_subtract_fusion.4), custom_call_target="Cholesky" | custom-call | tf_op jit(solution)/shard_map/cholesky/custom-call.3 | solution.py:10
  638.5 3.9 while.33
  642.5 19.9 %custom-call.33 = f32[2,128,128]{1,2,0:T(8,128)S(1)} custom-call(f32[2,128,128]{2,1,0:T(8,128)S(1)} %get-tuple-element.205), custom_call_target="InvertDiagBlocksLowerTriangular" | custom-call | tf_op jit(solution)/shard_map/triangular_solve/custom-call.0 | solution.py:11
  (371 shorter events, 157.9 us)
Async XLA Ops:
  8.0 134.9 %all-reduce.10.cloned.1.call-start = ((), (), s32[]{:S(2)}) async-start(), calls=%async_computation.5 | async-start | bytes 1048576 | tf_op jit(solution)/shard_map/psum | solution.py:82
  13.1 167.2 %all-gather.2.cloned.1.call-start = ((), (), s32[]{:S(2)}) async-start(), calls=%async_computation.1 | async-start | bytes 1310720 | tf_op jit(solution)/shard_map/all_gather | solution.py:90
  15.0 342.7 %all-reduce.6.cloned.1.call-start = ((), (), s32[]{:S(2)}) async-start(), calls=%async_computation.2 | async-start | bytes 1048576 | tf_op jit(solution)/shard_map/psum | solution.py:100
  302.7 104.3 %all-reduce.8.cloned.1.call-start = ((), (), s32[]{:S(2)}) async-start(), calls=%async_computation.3 | async-start | bytes 524288 | tf_op jit(solution)/shard_map/psum | solution.py:102
  361.3 49.2 %copy-start = (f32[128,512]{1,0:T(8,128)}, f32[128,512]{1,0:T(8,128)S(1)}, u32[]{:S(2)}) copy-start(f32[128,512]{1,0:T(8,128)S(1)} %fusion.48) | copy-start | bytes 786436
  362.2 48.4 %copy-start.1 = (f32[512,128]{0,1:T(8,128)}, f32[512,128]{0,1:T(8,128)S(1)}, u32[]{:S(2)}) copy-start(f32[512,128]{0,1:T(8,128)S(1)} %fusion.46) | copy-start | bytes 786436
  363.5 298.9 %reduce-scatter.2.cloned.1.call-start = ((), (), s32[]{:S(2)}) async-start(), calls=%async_computation.4 | async-start | bytes 2621440 | tf_op jit(solution)/shard_map/reduce_scatter | solution.py:111
Sparse Core Ops, SparseCore 0:
  15.2 127.6 all-reduce.9
Sparse Core Ops, SparseCore 1:
  16.0 28.4 all-gather.1
  302.7 54.8 all-reduce.5
  363.6 43.3 all-reduce.7
  598.7 35.2 reduce-scatter.1
where the time goes:
time: 684 us; the launch traced here: 676 us
  waiting for transfers between devices  191 us (28%)
  other arithmetic  163 us (24%)
  local copies, waits for them, and re-layouts  148 us (22%)
  matrix products  133 us (19%)
  between operations  19.6 us (3%)
  loops' own time  13.9 us (2%)
  blocking collectives  7.08 us (1%)
    psum x1, waiting for transfers between devices, on_device(): lax.psum((jnp.dot(b_factor.T, b_factor, precision=highest), jnp.dot(c_fac...  117 us
    another operation x13, other arithmetic, solve_rows(): factor_low = lax.linalg.cholesky(gram)  68.6 us
    reshape x12, local copies, waits for them, and re-layouts, one_step(): tensor_group.reshape(group_size, block_edge, block_edge, block_edge)  52.5 us
    dot_general x12, matrix products, one_step(): jnp.einsum('bijk,bikr->bjr', tensor_group.reshape(group_size, block_edge,...  48.5 us
    convert_element_type x12, other arithmetic, one_step(): (left_blk[:, :, None, :] * tail_blk[:, None, :, :]).astype(jnp.bfloat16)  46.2 us
    psum x1, waiting for transfers between devices, on_device(): gram_first = lax.psum(jnp.dot(a_whole.T, a_whole, precision=highest), 'grp')  43.4 us
    another operation x5, other arithmetic, solve_rows(): lax.linalg.triangular_solve(factor_low, right_side, left_side=False, lowe...  39.6 us
    gather x24, local copies, waits for them, and re-layouts, one_step(): left_blk = left_table[left_idx].astype(jnp.float32)  39.6 us
  transfers between devices with their start and end apart: 5, of which 3 were waited for; matrix products, arithmetic and copies ran while one was open for 19% of the time, Pallas kernels for 0%

commit v1 on v0

v1 whole, which is shorter than its diff:
```python
import functools
import jax
import jax.numpy as jnp
from jax import lax
from jax.experimental import pallas as pl
from jax.experimental.pallas import tpu as pltpu
from jax.sharding import PartitionSpec as P

HIGHEST = lax.Precision.HIGHEST
GROUP = 16
UNROLL = 2
QUARTER = 32
LANES = 128
VMEM_LIMIT = 56 * 1024 * 1024


def khatri_rao(left, tail, first):
    rows = [
        jnp.broadcast_to(left[first + t : first + t + 1, :], tail.shape).astype(jnp.bfloat16) * tail
        for t in range(8)
    ]
    return jnp.concatenate(rows, axis=0)


def product_rows(lhs_part, left, tail):
    total = None
    for q in range(4):
        term = jnp.dot(
            lhs_part(q), khatri_rao(left, tail, 8 * q), preferred_element_type=jnp.float32
        )
        total = term if total is None else total + term
    return total


def slot_loop(count, do_slot):
    base = pl.program_id(0) * GROUP
    steps = jnp.clip((count - base + UNROLL - 1) // UNROLL, 0, GROUP // UNROLL)

    def body(step, carry):
        for u in range(UNROLL):
            local = step * UNROLL + u
            do_slot(local, base + local, u)
        return carry

    lax.fori_loop(0, steps, body, 0)


def mode_one_kernel(i_ref, j_ref, k_ref, n_ref, x_ref, b_ref, c_ref, out_ref):
    @pl.when(pl.program_id(0) == 0)
    def _():
        out_ref[...] = jnp.zeros_like(out_ref)

    count = n_ref[0]

    def do_slot(local, slot, u):
        left = b_ref[pl.ds(pl.multiple_of(j_ref[slot] * 32, 32), 32), :].astype(jnp.float32)
        tail = c_ref[pl.ds(pl.multiple_of(k_ref[slot] * 32, 32), 32), :]
        result = product_rows(lambda q: x_ref[local, :, q * 256 : (q + 1) * 256], left, tail)
        alive = (slot < count).astype(jnp.float32)
        rows = pl.ds(pl.multiple_of(i_ref[slot] * 32, 32), 32)
        out_ref[rows, :] += result * alive

    slot_loop(count, do_slot)


def quarter_swap(parts):
    lane = lax.broadcasted_iota(jnp.int32, parts[0].shape, 1)
    even = (lane // QUARTER) % 2 == 0
    low = lane < 2 * QUARTER

    def pair(p, q, keep, dist):
        return (
            jnp.where(keep, p, pltpu.roll(q, dist, 1)),
            jnp.where(keep, pltpu.roll(p, LANES - dist, 1), q),
        )

    p0, p1 = pair(parts[0], parts[1], even, QUARTER)
    p2, p3 = pair(parts[2], parts[3], even, QUARTER)
    r0, r2 = pair(p0, p2, low, 2 * QUARTER)
    r1, r3 = pair(p1, p3, low, 2 * QUARTER)
    return [r0, r1, r2, r3]


def mode_two_kernel(i_ref, j_ref, k_ref, n_ref, x_ref, a_ref, c_ref, out_ref, wide):
    @pl.when(pl.program_id(0) == 0)
    def _():
        out_ref[...] = jnp.zeros_like(out_ref)

    count = n_ref[0]

    def do_slot(local, slot, u):
        for col in range(8):
            wide[u, 32 * col : 32 * col + 32, :] = x_ref[
                local, :, col * LANES : (col + 1) * LANES
            ].astype(jnp.float32)

        def lhs_part(q):
            pieces = []
            for half in range(2):
                first = q * 8 + half * 4
                parts = [wide[u, pl.ds(first + t, 8, stride=32), :] for t in range(4)]
                pieces.append(jnp.concatenate(quarter_swap(parts), axis=0).astype(jnp.bfloat16))
            return jnp.concatenate(pieces, axis=1)

        left = a_ref[pl.ds(pl.multiple_of(i_ref[slot] * 32, 32), 32), :].astype(jnp.float32)
        tail = c_ref[pl.ds(pl.multiple_of(k_ref[slot] * 32, 32), 32), :]
        result = product_rows(lhs_part, left, tail)
        alive = (slot < count).astype(jnp.float32)
        rows = pl.ds(pl.multiple_of(j_ref[slot] * 32, 32), 32)
        out_ref[rows, :] += result * alive

    slot_loop(count, do_slot)


def mode_call(kernel, scalars, blocks, left, tail, rows, scratch):
    slots, edge, width = blocks.shape
    rank = left.shape[1]
    grid_spec = pltpu.PrefetchScalarGridSpec(
        num_scalar_prefetch=4,
        grid=(slots // GROUP,),
        in_specs=[
            pl.BlockSpec((GROUP, edge, width), lambda g, *_: (g, 0, 0)),
            pl.BlockSpec(left.shape, lambda g, *_: (0, 0)),
            pl.BlockSpec(tail.shape, lambda g, *_: (0, 0)),
        ],
        out_specs=pl.BlockSpec((rows, rank), lambda g, *_: (0, 0)),
        scratch_shapes=scratch,
    )
    return pl.pallas_call(
        kernel,
        grid_spec=grid_spec,
        out_shape=jax.ShapeDtypeStruct((rows, rank), jnp.float32),
        compiler_params=pltpu.CompilerParams(vmem_limit_bytes=VMEM_LIMIT),
        cost_estimate=pl.CostEstimate(
            flops=2 * slots * edge * width * rank,
            bytes_accessed=2 * slots * edge * width,
            transcendentals=0,
        ),
    )(*scalars, blocks, left, tail)


def inverse_kernel(g_ref, out_ref):
    gram = g_ref[...]
    size = gram.shape[0]
    row = lax.broadcasted_iota(jnp.int32, gram.shape, 0)
    col = lax.broadcasted_iota(jnp.int32, gram.shape, 1)
    eye = (row == col).astype(jnp.float32)
    scale_row = lax.rsqrt(jnp.sum(gram * eye, axis=0, keepdims=True))
    scale_col = lax.rsqrt(jnp.sum(gram * eye, axis=1, keepdims=True))
    unit = gram * scale_row * scale_col
    bound = jnp.max(jnp.sum(jnp.abs(unit), axis=0, keepdims=True))

    def residual(x):
        return eye - jnp.dot(unit, x, precision=HIGHEST, preferred_element_type=jnp.float32)

    def update(x, r):
        return x + jnp.dot(x, r, precision=HIGHEST, preferred_element_type=jnp.float32)

    def more(state):
        step, worst, _, _ = state
        return jnp.logical_and(step < 60, worst > 1e-6)

    def body(state):
        step, _, x, r = state
        x = update(x, r)
        r = residual(x)
        return step + 1, jnp.sum(r * r), x, r

    x = eye * (1.0 / bound)
    r = residual(x)
    _, _, x, r = lax.while_loop(more, body, (jnp.int32(0), jnp.sum(r * r), x, r))
    out_ref[...] = update(x, r) * scale_row * scale_col


def inverse(gram):
    return pl.pallas_call(
        inverse_kernel,
        out_shape=jax.ShapeDtypeStruct(gram.shape, jnp.float32),
        in_specs=[pl.BlockSpec(memory_space=pltpu.VMEM)],
        out_specs=pl.BlockSpec(memory_space=pltpu.VMEM),
        compiler_params=pltpu.CompilerParams(vmem_limit_bytes=VMEM_LIMIT),
    )(gram)


def on_device(blocks, i_index, j_index, k_index, block_count, b_factor, c_factor):
    edge = blocks.shape[1]
    rank = b_factor.shape[1]
    gram_second, gram_third = lax.psum(
        (
            jnp.dot(b_factor.T, b_factor, precision=HIGHEST),
            jnp.dot(c_factor.T, c_factor, precision=HIGHEST),
        ),
        ("grp", "col"),
    )
    b_range = lax.all_gather(b_factor.astype(jnp.bfloat16), "grp", axis=0, tiled=True)
    c_range = lax.all_gather(c_factor.astype(jnp.bfloat16), "grp", axis=0, tiled=True)
    scalars = (i_index, j_index, k_index, block_count)
    own_rows = 2 * edge
    first_rows = own_rows * lax.axis_size("col")
    partial_one = mode_call(mode_one_kernel, scalars, blocks, b_range, c_range, first_rows, [])
    whole_sum = lax.psum(partial_one, "col")
    a_whole = jnp.dot(whole_sum, inverse(gram_second * gram_third), precision=HIGHEST)
    gram_first = lax.psum(jnp.dot(a_whole.T, a_whole, precision=HIGHEST), "grp")
    col_norm = jnp.sqrt(jnp.diagonal(gram_first) + 1e-06)
    a_range = (a_whole / col_norm[None, :]).astype(jnp.bfloat16)
    a_update = lax.dynamic_slice_in_dim(a_whole, lax.axis_index("col") * own_rows, own_rows, 0)
    gram_two = gram_first / (col_norm[:, None] * col_norm[None, :]) * gram_third
    inverse_two = inverse(gram_two)
    partial_two = mode_call(
        mode_two_kernel,
        scalars,
        blocks,
        a_range,
        c_range,
        b_range.shape[0],
        [pltpu.VMEM((UNROLL, 8 * edge, LANES), jnp.float32)],
    )
    own_two = lax.psum_scatter(partial_two, "grp", scatter_dimension=0, tiled=True)
    b_rows = jnp.dot(own_two, inverse_two, precision=HIGHEST)
    b_update = b_rows.reshape(-1, 4, 8, rank).swapaxes(1, 2).reshape(b_rows.shape)
    return (a_update, b_update)


def solution(mesh):
    return jax.shard_map(
        on_device,
        mesh=mesh,
        in_specs=(
            P(("grp", "col"), None, None),
            P(("grp", "col")),
            P(("grp", "col")),
            P(("grp", "col")),
            P(("grp", "col")),
            P(("grp", "col"), None),
            P(("grp", "col"), None),
        ),
        out_specs=(P(("grp", "col"), None), P(("grp", "col"), None)),
        check_vma=False,
    )
```

time: 684 us -> 353 us (0.52)
  other arithmetic: 163 us -> 6.08 us
  local copies, waits for them, and re-layouts: 148 us -> 4.47 us
  matrix products: 133 us -> 10.1 us
  Pallas kernels: 0 us -> 66.8 us
  waiting for transfers between devices: 191 us -> 236 us
  loops' own time: 13.9 us -> 0 us
    dot_general x51 -> x5, matrix products: 122 us -> 10.1 us  [the longest x1 2.9 us: on_device(): jnp.dot(b_factor.T, b_factor, precision=HIGHEST)]
    another operation x20 -> x0, other arithmetic: 109 us -> none  [the longest x13 68.6 us: solve_rows(): factor_low = lax.linalg.cholesky(gram)]
    pallas_call x0 -> x4, Pallas kernels: none -> 66.8 us  [the longest x2 44.9 us: mode_call(): pl.pallas_call(kernel, grid_spec=grid_spec, out_shape=jax.ShapeDtypeStruc...]
    reshape x17 -> x1, local copies, waits for them, and re-layouts: 57.2 us -> 0.97 us  [on_device(): b_rows.reshape(-1, 4, 8, rank).swapaxes(1, 2).reshape(b_rows.shape)]
    gather x48 -> x0, local copies, waits for them, and re-layouts: 53.1 us -> none  [the longest x24 39.6 us: one_step(): left_blk = left_table[left_idx].astype(jnp.float32)]
    convert_element_type x61 -> x0, other arithmetic: 48.1 us -> none  [the longest x12 46.2 us: one_step(): (left_blk[:, :, None, :] * tail_blk[:, None, :, :]).astype(jnp.bfloat16)]
    reduce_scatter x1, waiting for transfers between devices: 0.03 us -> 47 us  [on_device(): lax.psum_scatter(partial_two, 'grp', scatter_dimension=0, tiled=True)]
    psum x3, waiting for transfers between devices: 191 us -> 174 us  [the longest x1 87.4 us: on_device(): lax.psum((jnp.dot(b_factor.T, b_factor, precision=HIGHEST), jnp.dot(c_fac...]
  transfers between devices with their start and end apart: 5 -> 5, of which waited for: 3 -> 5; matrix products, arithmetic and copies ran while one was open for 19% -> 3% of each run, Pallas kernels for 0% -> 12%
where the time goes in v1:
time: 353 us; the launch traced here: 349 us
  waiting for transfers between devices  236 us (67%)
  Pallas kernels  66.8 us (19%)
  between operations  15.9 us (5%)
  matrix products  10.1 us (3%)
  blocking collectives  9.33 us (3%)
  other arithmetic  6.08 us (2%)
  local copies, waits for them, and re-layouts  4.47 us (1%)
    psum x1, waiting for transfers between devices, on_device(): lax.psum((jnp.dot(b_factor.T, b_factor, precision=HIGHEST), jnp.dot(c_fac...  87.4 us
    reduce_scatter x1, waiting for transfers between devices, on_device(): lax.psum_scatter(partial_two, 'grp', scatter_dimension=0, tiled=True)  47 us
    pallas_call x2, Pallas kernels, mode_call(): pl.pallas_call(kernel, grid_spec=grid_spec, out_shape=jax.ShapeDtypeStruc...  44.9 us
    psum x1, waiting for transfers between devices, on_device(): gram_first = lax.psum(jnp.dot(a_whole.T, a_whole, precision=HIGHEST), 'grp')  43.9 us
    psum x1, waiting for transfers between devices, on_device(): whole_sum = lax.psum(partial_one, 'col')  43.1 us
    pallas_call x2, Pallas kernels, inverse(): pl.pallas_call(inverse_kernel, out_shape=jax.ShapeDtypeStruct(gram.shape,...  21.9 us
    all_gather x1, waiting for transfers between devices, on_device(): lax.all_gather(b_factor.astype(jnp.bfloat16), 'grp', axis=0, tiled=True)  14.8 us
    all_gather x1, blocking collectives, on_device(): lax.all_gather(c_factor.astype(jnp.bfloat16), 'grp', axis=0, tiled=True)  9.33 us
  transfers between devices with their start and end apart: 5, of which 5 were waited for; matrix products, arithmetic and copies ran while one was open for 3% of the time, Pallas kernels for 12%

profile of v1, /device:TPU:9, one launch (start us, length us, event | category | flops | bytes accessed | tf_op | source)
XLA Modules:
  0.0 349.2 jit_solution(10333785912418410346)
XLA Ops:
  8.0 0.0 all-gather.2.cloned.1.call-start
  8.0 1.8 convert_element_type.9
  9.8 0.0 all-gather.2.cloned.1.call-update
  9.8 0.0 all-reduce.9.cloned.1.call-start
  9.9 2.1 fusion.1
  12.0 2.9 fusion
  14.9 0.0 all-reduce.9.cloned.1.call-update
  14.9 0.0 all-reduce.5.cloned.1.call-start
  15.0 0.9 convert_element_type.10
  16.5 9.3 %all_gather.7.c_ref = bf16[512,256]{1,0:T(8,128)(2,1)} all-gather(bf16[128,256]{1,0:T(8,128)(2,1)S(1)} %convert_element_type.10), channel_id=1, replica_groups=mesh['grp'=4,'col'=8] {'grp'}, dimensions={0}, use_global_device_ids=true | all-gather | bytes 327680 | tf_op jit(solution)/shard_map/all_gather | solution.py:196
  25.9 14.8 %all-gather.2.cloned.1.call-done.b_ref = bf16[2048,256]{1,0:T(8,128)(2,1)} async-done(((bf16[512,256]{1,0:T(8,128)(2,1)}), bf16[2048,256]{1,0:T(8,128)(2,1)}) %all-gather.2.cloned.1.call-update) | async-done | bytes 1048592 | tf_op jit(solution)/shard_map/all_gather | solution.py:195
  40.6 18.6 %shard_map.86 = f32[512,256]{1,0:T(8,128)} custom-call(s32[192]{0:T(256)} %i_ref.3, s32[192]{0:T(256)} %j_ref.3, s32[192]{0:T(256)} %k_ref.3, s32[1]{0:T(128)S(6)} %copy.15.n_ref, bf16[192,32,1024]{2,1,0:T(8,128)(2,1)} %x_ref.3, bf16[2048,256]{1,0:T(8,128)(2,1)} %all-gather.2.cloned.1.call-done.b_ref, bf16[512,256]{1,0:T(8,128)(2,1)} %all_gather.7.c_ref), custom_call_target="tpu_custom_call" | custom-call | flops 3221225472 | bytes 12582912 | tf_op jit(solution)/shard_map/pallas_call | solution.py:129
  59.2 0.0 all-reduce.5.cloned.1.call-update
  59.2 0.0 all-reduce.7.cloned.1.call-start
  59.3 87.4 %all-reduce.9.cloned.1.call-done = (f32[256,256]{1,0:T(8,128)}, f32[256,256]{1,0:T(8,128)}) async-done(((f32[256,256]{1,0:T(8,128)}, f32[256,256]{1,0:T(8,128)}), (f32[256,256]{1,0:T(8,128)}, f32[256,256]{1,0:T(8,128)})) %all-reduce.9.cloned.1.call-update) | async-done | bytes 524304 | tf_op jit(solution)/shard_map/psum | solution.py:188
  146.7 0.0 copy-start.1
  146.7 1.8 mul.22.g_ref
  148.5 12.8 %shard_map.87 = f32[256,256]{1,0:T(8,128)} custom-call(f32[256,256]{1,0:T(8,128)} %mul.22.g_ref), custom_call_target="tpu_custom_call" | custom-call | tf_op jit(solution)/shard_map/pallas_call | solution.py:176
  161.3 43.1 %all-reduce.5.cloned.1.call-done = f32[512,256]{1,0:T(8,128)} async-done(((f32[512,256]{1,0:T(8,128)}), f32[512,256]{1,0:T(8,128)}) %all-reduce.5.cloned.1.call-update) | async-done | bytes 524304 | tf_op jit(solution)/shard_map/psum | solution.py:201
  204.4 1.7 fusion.2
  206.1 1.7 fusion.3
  207.8 0.0 all-reduce.7.cloned.1.call-update
  207.8 0.0 reduce-scatter.2.cloned.1.call-start
  207.9 43.9 %all-reduce.7.cloned.1.call-done = f32[256,256]{1,0:T(8,128)} async-done(((f32[256,256]{1,0:T(8,128)}), f32[256,256]{1,0:T(8,128)}) %all-reduce.7.cloned.1.call-update) | async-done | bytes 262160 | tf_op jit(solution)/shard_map/psum | solution.py:203
  251.8 0.0 copy-start
  251.8 2.6 gather_fusion
  254.4 0.8 divide_convert_fusion.a_ref
  255.2 26.4 %shard_map.88 = f32[2048,256]{1,0:T(8,128)} custom-call(s32[192]{0:T(256)} %i_ref.3, s32[192]{0:T(256)} %j_ref.3, s32[192]{0:T(256)} %k_ref.3, s32[1]{0:T(128)S(6)} %copy.15.n_ref, bf16[192,32,1024]{2,1,0:T(8,128)(2,1)} %x_ref.3, bf16[512,256]{1,0:T(8,128)(2,1)} %divide_convert_fusion.a_ref, bf16[512,256]{1,0:T(8,128)(2,1)} %all_gather.7.c_ref), custom_call_target="tpu_custom_call" | custom-call | flops 3221225472 | bytes 12582912 | tf_op jit(solution)/shard_map/pallas_call | solution.py:129
  281.6 0.0 reduce-scatter.2.cloned.1.call-update
  281.6 0.6 constant_dynamic-slice_fusion
  282.2 0.0 copy-done.1
  282.2 0.0 copy-done
  282.2 0.8 divide_multiply_fusion.g_ref
  283.0 9.1 %shard_map.89 = f32[256,256]{1,0:T(8,128)} custom-call(f32[256,256]{1,0:T(8,128)} %divide_multiply_fusion.g_ref), custom_call_target="tpu_custom_call" | custom-call | tf_op jit(solution)/shard_map/pallas_call | solution.py:176
  292.1 47.0 %reduce-scatter.2.cloned.1.call-done = f32[512,256]{1,0:T(8,128)} async-done(((f32[2048,256]{1,0:T(8,128)}), f32[512,256]{1,0:T(8,128)}) %reduce-scatter.2.cloned.1.call-update) | async-done | bytes 524304 | tf_op jit(solution)/shard_map/reduce_scatter | solution.py:218
  339.2 1.7 fusion.4
  340.9 0.2 copy.10
  341.1 1.0 reshape.19
  (2 shorter events, 0.0 us)
Async XLA Ops:
  8.0 32.6 %all-gather.2.cloned.1.call-start = ((), (), s32[]{:S(2)}) async-start(), calls=%async_computation.1 | async-start | bytes 1310720 | tf_op jit(solution)/shard_map/all_gather | solution.py:195
  9.8 136.8 %all-reduce.9.cloned.1.call-start = ((), (), s32[]{:S(2)}) async-start(), calls=%async_computation.5 | async-start | bytes 1048576 | tf_op jit(solution)/shard_map/psum | solution.py:188
  14.9 189.5 %all-reduce.5.cloned.1.call-start = ((), (), s32[]{:S(2)}) async-start(), calls=%async_computation.2 | async-start | bytes 1048576 | tf_op jit(solution)/shard_map/psum | solution.py:201
  59.2 192.6 %all-reduce.7.cloned.1.call-start = ((), (), s32[]{:S(2)}) async-start(), calls=%async_computation.3 | async-start | bytes 524288 | tf_op jit(solution)/shard_map/psum | solution.py:203
  146.7 135.5 %copy-start.1 = (f32[256,256]{1,0:T(8,128)S(1)}, f32[256,256]{1,0:T(8,128)}, u32[]{:S(2)}) copy-start(f32[256,256]{1,0:T(8,128)} %get-tuple-element.3) | copy-start | bytes 786436
  207.8 131.3 %reduce-scatter.2.cloned.1.call-start = ((), (), s32[]{:S(2)}) async-start(), calls=%async_computation.4 | async-start | bytes 2621440 | tf_op jit(solution)/shard_map/reduce_scatter | solution.py:218
  251.8 30.4 %copy-start = (f32[256,256]{1,0:T(8,128)S(1)}, f32[256,256]{1,0:T(8,128)}, u32[]{:S(2)}) copy-start(f32[256,256]{1,0:T(8,128)} %all-reduce.7.cloned.1.call-done) | copy-start | bytes 786436
Sparse Core Ops, SparseCore 0:
  11.4 29.1 all-gather.1
  208.0 43.7 all-reduce.6
  281.7 57.4 reduce-scatter.1
Sparse Core Ops, SparseCore 1:
  15.8 130.9 all-reduce.8
  149.6 54.8 all-reduce.4
